TPU v7x, 32 devices: a whole 2x2x4 slice. The times are simulated.
32 devices in a mesh: draws: 2 (over y), dst: 4 (over z), org: 2 (over x), st: 2 (over core).
Axes of the slice: x: 2, y: 2, z: 4, core: 2. Of those that a mesh axis runs over, the one named last changes fastest.
Arguments:
- value_now: float32 [8, 2, 64, 4096], P(('draws', 'dst'), 'org', None, 'st'), parts along dimension 0, may hold values from -90 to 490
- utility: float32 [8, 2, 64, 4096], P(('draws', 'dst'), 'org', None, 'st'), parts along dimension 0, may hold values from -6 to 6
- move_costs: float32 [8, 2, 64, 4, 128], P('draws', 'org', None, 'dst'), parts along dimension 0, may hold values from 0 to 3
- dest_blocks: int32 [8, 3], replicated, may hold values from 0 to 7, all different within a row
- row_counts: int32 [8], replicated, may hold values from 1 to 3, as said below
- transition: int32 [4096], replicated, may hold values from 0 to 4095
Outputs:
- value_next: float32 [8, 2, 64, 4096], P(('draws', 'dst'), 'org', None, 'st'), parts along dimension 0
There are 2 independent parts, one for each index of `draws`. A program takes and returns all parts, laid end to end along the dimension named above; an argument that names none is the same for every part. Nothing has to cross between parts.
Inputs may be any that keep to these rules, and one draw needn't show every extreme that they name: `dest_blocks`: each row names 3 different blocks; only the first row_counts[o] of row o count. `row_counts`: some anchor block has 3.
All inputs are finite; a program needn't handle non-finite values.
Results may differ from a plain program's by a relative error of at most 0.00095.
Values may be sent and summed in bfloat16 or wider, within the bound.
A program may use at most 64 MiB of HBM per device.

v0:
```python
import jax
import jax.numpy as jnp
from jax import lax
from jax.sharding import PartitionSpec as P

DISCOUNT = 0.95
FLOOR = -1e30


def block_terms(kernel, feasible, ceiling, dest_piece):
    pieces = dest_piece.shape[0]
    block_rows = dest_piece.shape[1]
    states = dest_piece.shape[2]
    dest_rows = dest_piece.reshape(pieces * block_rows, states)

    def dense_anchor(operands):
        kernel_row, usable_row, ceiling_row = operands
        keep_mask = jnp.broadcast_to(usable_row[:, None], (pieces, block_rows)).reshape(
            pieces * block_rows, 1
        )
        weights = jnp.where(keep_mask, jnp.exp(dest_rows - ceiling_row[None, :]), 0.0).astype(
            jnp.bfloat16
        )
        return jnp.dot(kernel_row, weights, preferred_element_type=jnp.float32)

    return lax.map(dense_anchor, (kernel, feasible, ceiling))


def on_device(value_now, utility, move_costs, dest_blocks, row_counts, transition):
    dest_groups = lax.axis_size("dst")
    orig_groups = lax.axis_size("org")
    dest_index = lax.axis_index("dst")
    orig_index = lax.axis_index("org")
    state_index = lax.axis_index("st")
    states = value_now.shape[3]
    slot_count = dest_blocks.shape[1]
    every_state = lax.all_gather(value_now, "st", axis=3, tiled=True)
    chosen = lax.dynamic_slice_in_dim(transition, state_index * states, states)
    shifted = jnp.take(every_state, chosen, axis=3)
    own_piece = shifted[0]
    kernel = jnp.exp(-move_costs[:, 0, :, 0, :]).astype(jnp.bfloat16)
    lists_by = dest_blocks.reshape(dest_groups, orig_groups, slot_count)
    counts_by = row_counts.reshape(dest_groups, orig_groups)
    lists_mine = lax.dynamic_index_in_dim(lists_by, orig_index, 1, keepdims=False)
    counts_mine = lax.dynamic_index_in_dim(counts_by, orig_index, 1, keepdims=False)
    slot_ids = jnp.arange(slot_count, dtype=jnp.int32)
    usable = slot_ids[None, :] < counts_mine[:, None]
    dest_ids = dest_index * orig_groups + jnp.arange(orig_groups, dtype=jnp.int32)
    feasible = jnp.any(
        (lists_mine[:, :, None] == dest_ids[None, None, :]) & usable[:, :, None], axis=1
    )
    own_id = dest_index * orig_groups + orig_index
    slot_live = slot_ids[None, :] < row_counts[:, None]
    reaches = jnp.any((dest_blocks == own_id) & slot_live, axis=1)
    own_top = jnp.max(own_piece[0], axis=0)
    offered = jnp.where(reaches[:, None], own_top[None, :], FLOOR)
    every_top = lax.pmax(offered.astype(jnp.bfloat16), ("dst", "org")).astype(offered.dtype)
    ceiling = lax.dynamic_index_in_dim(
        every_top.reshape(dest_groups, orig_groups, states), orig_index, 1, keepdims=False
    )
    partial_value = block_terms(
        kernel, feasible, ceiling, lax.all_gather(own_piece, "org", axis=0, tiled=True)
    )
    rounded = partial_value.astype(jnp.bfloat16)
    merged = jnp.sum(
        lax.all_to_all(rounded, "dst", split_axis=0, concat_axis=0, tiled=True),
        axis=0,
        dtype=jnp.float32,
    )
    own_ceiling = lax.dynamic_index_in_dim(ceiling, dest_index, 0, keepdims=False)
    result = utility[0, 0] + DISCOUNT * (own_ceiling[None, :] + jnp.log(merged))
    return result[None, None]


def solution(mesh):
    return jax.shard_map(
        on_device,
        mesh=mesh,
        in_specs=(
            P(("draws", "dst"), "org", None, "st"),
            P(("draws", "dst"), "org", None, "st"),
            P("draws", "org", None, "dst", None),
            P(),
            P(),
            P(),
        ),
        out_specs=P(("draws", "dst"), "org", None, "st"),
        check_vma=False,
    )
```

profile of v0, /device:TPU:0, one launch (start us, length us, event | category | flops | bytes accessed | tf_op | source)
XLA Modules:
  0.0 111.2 jit_solution(2827117173432948598)
XLA Ops:
  6.5 0.0 copy-start.4
  6.5 0.0 copy-start.3
  6.5 0.0 copy-start.2
  6.5 0.0 all-gather.3.cloned.1.call-start
  6.5 2.4 %copy.18 = f32[1,1,64,2048]{2,3,1,0:T(8,128)} copy(f32[1,1,64,2048]{3,2,1,0:T(8,128)} %param.8) | data formatting | bytes 1048576 | tf_op args[0]
  8.9 0.0 all-gather.3.cloned.1.call-update
  9.0 0.0 all-gather.5.cloned.1.call-start
  9.0 0.0 copy-done.4
  9.1 0.1 reshape.142
  9.1 0.0 copy-done.3
  9.1 0.1 copy.20
  9.2 0.2 dynamic-slice_reduce_fusion
  9.4 0.0 copy-done.2
  9.5 0.1 iota_compare_fusion
  9.6 0.2 and_reduce_fusion
  9.8 12.6 %all-gather.3.cloned.1.call-done = f32[1,1,64,4096]{2,3,1,0:T(8,128)} async-done(((f32[1,1,64,2048]{2,3,1,0:T(8,128)}), f32[1,1,64,4096]{2,3,1,0:T(8,128)}) %all-gather.3.cloned.1.call-update) | async-done | bytes 1048592 | tf_op jit(solution)/shard_map/all_gather | solution.py:37
  22.4 7.0 %gather_fusion = f32[2048,64]{1,0:T(8,128)S(1)} fusion(f32[64,4096]{0,1:T(8,128)} %bitcast.42, s32[2048]{0:T(1024)S(1)} %fusion.12), kind=kCustom, calls=%fused_computation | custom fusion | bytes 1056768 | tf_op jit(solution)/shard_map/jit(_take)/gather | solution.py:39
  29.5 0.0 copy-start.1
  29.5 0.3 bitcast_select_fusion
  29.8 1.1 %copy.21 = f32[1,64,2048]{2,1,0:T(8,128)} copy(f32[1,64,2048]{1,2,0:T(8,128)S(1)} %bitcast_select_fusion) | data formatting | bytes 1048576 | tf_op jit(solution)/shard_map/jit(_take)/select_n | solution.py:39
  30.9 0.0 all-gather.5.cloned.1.call-update
  31.0 0.0 copy-done.1
  31.0 0.6 fusion.8
  31.6 0.1 select_convert_fusion.2
  31.8 37.6 %pmax.7 = bf16[4,2,2048]{2,1,0:T(2,128)(2,1)S(1)} all-reduce(bf16[4,2,2048]{2,1,0:T(2,128)(2,1)S(1)} %reshape.139), channel_id=1, replica_groups=mesh['draws'=2,'dst'=4,'org'=2,'st'=2] {'dst','org'}, use_global_device_ids=true, to_apply=%region_2.3 | all-reduce | flops 16384 | bytes 65536 | tf_op jit(solution)/shard_map/pmax | solution.py:57
  69.4 0.0 all-gather.5.cloned.1.call-done
  69.4 10.5 %while.10 = (s32[]{:T(128)}, bf16[4,64,2048]{2,1,0:T(8,128)(2,1)}, bf16[4,64,128]{2,1,0:T(8,128)(2,1)S(1)}, pred[4,2]{0,1:T(4,128)(4,1)S(1)}, f32[4,2048]{1,0:T(4,128)S(1)}, /*index=5*/f32[128,2048]{1,0:T(8,128)}, s32[]{:T(128)}) while((s32[]{:T(128)}, bf16[4,64,2048]{2,1,0:T(8,128)(2,1)}, bf16[4,64,128]{2,1,0:T(8,128)(2,1)S(1)}, ...), condition=%wide.region_5.6_spmd, body=%wide.region_4.5_spmd.sunk | while | flops 34340864 | bytes 1615847 | solution.py:26
  69.5 0.1 constant_dynamic-slice_fusion.8
  69.5 0.1 copy.28
  69.6 0.1 broadcast_in_dim.107
  69.7 0.1 broadcast_in_dim.108
  69.8 2.3 %fusion.18 = bf16[4,64,2048]{2,1,0:T(8,128)(2,1)} fusion(bf16[4,64,2048]{2,1,0:T(8,128)(2,1)} %get-tuple-element.101, s32[]{:T(128)S(6)} %copy.32, f32[128,2048]{1,0:T(8,128)} %get-tuple-element.112, f32[2048]{0:T(1024)S(1)} %bitcast.43, pred[128]{0:T(512)(128)(4,1)S(1)} %broadcast_in_dim.108, bf16[4,64,128]{2,1,0:T(8,128)(2,1)S(1)} %get-tuple-element.109), kind=kOutput, calls=%fused_computation.2.clone.1 | convolution fusion | flops 34340864 | bytes 1598976 | tf_op jit(solution)/shard_map/while/body/eval_jaxpr/dot_general | solution.py:24
  72.1 0.1 constant_dynamic-slice_fusion.8
  72.2 0.1 copy.28
  72.3 0.1 broadcast_in_dim.107
  72.3 0.1 broadcast_in_dim.108
  72.4 2.2 %fusion.18 = bf16[4,64,2048]{2,1,0:T(8,128)(2,1)} fusion(bf16[4,64,2048]{2,1,0:T(8,128)(2,1)} %get-tuple-element.101, s32[]{:T(128)S(6)} %copy.32, f32[128,2048]{1,0:T(8,128)} %get-tuple-element.112, f32[2048]{0:T(1024)S(1)} %bitcast.43, pred[128]{0:T(512)(128)(4,1)S(1)} %broadcast_in_dim.108, bf16[4,64,128]{2,1,0:T(8,128)(2,1)S(1)} %get-tuple-element.109), kind=kOutput, calls=%fused_computation.2.clone.1 | convolution fusion | flops 34340864 | bytes 1598976 | tf_op jit(solution)/shard_map/while/body/eval_jaxpr/dot_general | solution.py:24
  74.7 0.1 constant_dynamic-slice_fusion.8
  74.8 0.1 copy.28
  74.9 0.1 broadcast_in_dim.107
  74.9 0.1 broadcast_in_dim.108
  75.0 2.2 %fusion.18 = bf16[4,64,2048]{2,1,0:T(8,128)(2,1)} fusion(bf16[4,64,2048]{2,1,0:T(8,128)(2,1)} %get-tuple-element.101, s32[]{:T(128)S(6)} %copy.32, f32[128,2048]{1,0:T(8,128)} %get-tuple-element.112, f32[2048]{0:T(1024)S(1)} %bitcast.43, pred[128]{0:T(512)(128)(4,1)S(1)} %broadcast_in_dim.108, bf16[4,64,128]{2,1,0:T(8,128)(2,1)S(1)} %get-tuple-element.109), kind=kOutput, calls=%fused_computation.2.clone.1 | convolution fusion | flops 34340864 | bytes 1598976 | tf_op jit(solution)/shard_map/while/body/eval_jaxpr/dot_general | solution.py:24
  77.3 0.1 constant_dynamic-slice_fusion.8
  77.4 0.1 copy.28
  77.5 0.1 broadcast_in_dim.107
  77.5 0.1 broadcast_in_dim.108
  77.6 2.3 %fusion.18 = bf16[4,64,2048]{2,1,0:T(8,128)(2,1)} fusion(bf16[4,64,2048]{2,1,0:T(8,128)(2,1)} %get-tuple-element.101, s32[]{:T(128)S(6)} %copy.32, f32[128,2048]{1,0:T(8,128)} %get-tuple-element.112, f32[2048]{0:T(1024)S(1)} %bitcast.43, pred[128]{0:T(512)(128)(4,1)S(1)} %broadcast_in_dim.108, bf16[4,64,128]{2,1,0:T(8,128)(2,1)S(1)} %get-tuple-element.109), kind=kOutput, calls=%fused_computation.2.clone.1 | convolution fusion | flops 34340864 | bytes 1598976 | tf_op jit(solution)/shard_map/while/body/eval_jaxpr/dot_general | solution.py:24
  79.9 0.0 copy-start
  79.9 3.6 %all-to-all-start = ((bf16[4,64,2048]{2,1,0:T(8,128)(2,1)}), bf16[4,64,2048]{2,1,0:T(8,128)(2,1)S(1)}, u32[]{:S(2)}, u32[]{:S(2)}) async-start(bf16[4,64,2048]{2,1,0:T(8,128)(2,1)} %get-tuple-element.37), calls=%async_computation | async-start | bytes 2097152 | tf_op jit(solution)/shard_map/all_to_all | solution.py:66
  83.6 19.7 %all-to-all-done = bf16[4,64,2048]{2,1,0:T(8,128)(2,1)S(1)} async-done(((bf16[4,64,2048]{2,1,0:T(8,128)(2,1)}), bf16[4,64,2048]{2,1,0:T(8,128)(2,1)S(1)}, u32[]{:S(2)}, u32[]{:S(2)}) %all-to-all-start) | async-done | bytes 1048608 | tf_op jit(solution)/shard_map/all_to_all | solution.py:66
  103.3 0.2 convert_reduce_fusion
  103.4 0.0 copy-done
  103.5 0.9 fusion.10
  (16 shorter events, 0.3 us)
Async XLA Ops:
  6.5 2.5 %copy-start.4 = (s32[8]{0:T(128)S(1)}, s32[8]{0:T(128)}, u32[]{:S(2)}) copy-start(s32[8]{0:T(128)} %param.12) | copy-start | bytes 100
  6.5 2.6 %copy-start.3 = (s32[8,3]{0,1:T(4,128)S(1)}, s32[8,3]{0,1:T(4,128)}, u32[]{:S(2)}) copy-start(s32[8,3]{0,1:T(4,128)} %param.11) | copy-start | bytes 292
  6.5 2.9 %copy-start.2 = (s32[4096]{0:T(1024)S(1)}, s32[4096]{0:T(1024)}, u32[]{:S(2)}) copy-start(s32[4096]{0:T(1024)} %param.13) | copy-start | bytes 49156
  6.5 15.9 %all-gather.3.cloned.1.call-start = ((), (), s32[]{:S(2)}) async-start(), calls=%async_computation.1 | async-start | bytes 3145728 | tf_op jit(solution)/shard_map/all_gather | solution.py:37
  9.0 60.5 %all-gather.5.cloned.1.call-start = ((), (), s32[]{:S(2)}) async-start(), calls=%async_computation.2 | async-start | bytes 1572864 | tf_op jit(solution)/shard_map/all_gather | solution.py:62
  29.5 1.5 %copy-start.1 = (f32[4,1,64,1,128]{4,3,2,1,0:T(1,128)S(1)}, f32[4,1,64,1,128]{4,3,2,1,0:T(1,128)}, u32[]{:S(2)}) copy-start(f32[4,1,64,1,128]{4,3,2,1,0:T(1,128)} %param.10) | copy-start | bytes 393220
  79.9 23.5 %copy-start = (f32[1,1,64,2048]{3,2,1,0:T(8,128)S(1)}, f32[1,1,64,2048]{3,2,1,0:T(8,128)}, u32[]{:S(2)}) copy-start(f32[1,1,64,2048]{3,2,1,0:T(8,128)} %param.9) | copy-start | bytes 1572868
  79.9 23.4 %all-to-all-start = ((bf16[4,64,2048]{2,1,0:T(8,128)(2,1)}), bf16[4,64,2048]{2,1,0:T(8,128)(2,1)S(1)}, u32[]{:S(2)}, u32[]{:S(2)}) async-start(bf16[4,64,2048]{2,1,0:T(8,128)(2,1)} %get-tuple-element.37), calls=%async_computation | async-start | bytes 2097152 | tf_op jit(solution)/shard_map/all_to_all | solution.py:66
Sparse Core Ops, SparseCore 0:
  9.1 13.2 all-gather.2
  31.1 22.9 all-gather.4
where the time goes:
time: 112 us; the launch traced here: 111 us
  blocking collectives  37.6 us (34%)
  waiting for transfers between devices  32.4 us (29%)
  between operations  13.6 us (12%)
  local copies, waits for them, and re-layouts  12.5 us (11%)
  matrix products  8.98 us (8%)
  starting transfers between devices  3.69 us (3%)
  other arithmetic  2.52 us (2%)
    pmax x1, blocking collectives, on_device(): lax.pmax(offered.astype(jnp.bfloat16), ('dst', 'org')).astype(offered.dtype)  37.6 us
    all_to_all x1, waiting for transfers between devices, on_device(): lax.all_to_all(rounded, 'dst', split_axis=0, concat_axis=0, tiled=True)  19.7 us
    all_gather x1, waiting for transfers between devices, on_device(): every_state = lax.all_gather(value_now, 'st', axis=3, tiled=True)  12.6 us
    dot_general x4, matrix products, dense_anchor(): return jnp.dot(kernel_row, weights, preferred_element_type=jnp.float32)  8.98 us
    gather x1, local copies, waits for them, and re-layouts, on_device(): shifted = jnp.take(every_state, chosen, axis=3)  7.05 us
    all_to_all x1, starting transfers between devices, on_device(): lax.all_to_all(rounded, 'dst', split_axis=0, concat_axis=0, tiled=True)  3.65 us
    unnamed x13, local copies, waits for them, and re-layouts  2.52 us
  transfers between devices with their start and end apart: 3, of which 2 were waited for; matrix products, arithmetic and copies ran while one was open for 1% of the time, Pallas kernels for 0%

commit v1 on v0

v1 whole, which is shorter than its diff:
```python
import functools

import jax
import jax.numpy as jnp
from jax import lax
from jax.experimental import pallas as pl
from jax.experimental.pallas import tpu as pltpu
from jax.sharding import PartitionSpec as P

DISCOUNT = 0.95
FLOOR = -1e30
TILE = 256
CHUNK = 512
AHEAD = 2
MESH = pl.DeviceIdType.MESH


def sweep(
    sizes, v_ref, cost_ref, trans_ref, lists_ref, counts_ref, out_ref,
    raw, raw_top, kern_out, kern_in, onehot, wbuf, tops, own_sum, own_top,
    x_out, x_out_top, x_in, x_in_top, reach,
    st_send, st_recv, k_send, k_recv, t_send, t_recv, up_send, dn_send, w_recv, x_send, x_recv,
):
    n_dst, n_org, n_st = sizes
    rows, states = v_ref.shape
    tiles = states // TILE
    chunks, width = wbuf.shape[1], wbuf.shape[3]
    slots = lists_ref.shape[1]
    p = lax.axis_index("dst")
    q = lax.axis_index("org")
    h = lax.axis_index("st")

    def remote(source, target, send, recv, **where):
        return pltpu.make_async_remote_copy(
            src_ref=source, dst_ref=target, send_sem=send, recv_sem=recv,
            device_id=where, device_id_type=MESH,
        )

    peers = [(a, b) for a in range(n_dst) for b in range(n_org) if (a, b) != (0, 0)]
    barrier = pltpu.get_barrier_semaphore()
    for dp, dq in peers:
        pl.semaphore_signal(
            barrier, inc=1, device_id_type=MESH,
            device_id={"dst": lax.rem(p + dp, n_dst), "org": lax.rem(q + dq, n_org)},
        )
    for d in range(1, n_st):
        pl.semaphore_signal(
            barrier, inc=1, device_id_type=MESH, device_id={"st": lax.rem(h + d, n_st)}
        )

    for t in range(tiles):
        x = v_ref[:, t * TILE:(t + 1) * TILE]
        top = jnp.max(x, axis=0, keepdims=True).astype(jnp.bfloat16).astype(jnp.float32)
        raw[h, t] = jnp.exp(x - top).astype(jnp.bfloat16)
        raw_top[h, t:t + 1, :] = top

    pl.semaphore_wait(barrier, len(peers) + n_st - 1)

    st_copies = []
    for d in range(1, n_st):
        other = lax.rem(h + d, n_st)
        for i, buf in enumerate((raw_top, raw)):
            st_copies.append(remote(
                buf.at[h], buf.at[h], st_send.at[d - 1, i], st_recv.at[d - 1, i], st=other))
            st_copies[-1].start()

    for a in range(n_dst):
        k = jnp.exp(-cost_ref[a]).astype(jnp.bfloat16)
        for b in range(n_org):
            kern_out[a, b] = k[:, b * rows:(b + 1) * rows]
    k_copies = []
    for i, (dp, dq) in enumerate(peers):
        to_p, to_q = lax.rem(p + dp, n_dst), lax.rem(q + dq, n_org)
        k_copies.append(remote(
            kern_out.at[to_p, to_q], kern_in.at[p, (n_org - dq) % n_org],
            k_send.at[i], k_recv.at[i], dst=to_p, org=to_q))
        k_copies[-1].start()
    kern_in[p, 0] = kern_out[p, q]

    for r in range(n_org):
        anchor = p * n_org + lax.rem(q + r, n_org)
        count = counts_ref[anchor]
        for b in range(n_dst):
            block = b * n_org + q

            def listed(k, found, anchor=anchor, block=block, count=count):
                hit = jnp.where(lists_ref[anchor, k] == block, 1, 0)
                return found + hit * jnp.where(k < count, 1, 0)

            if slots <= 4:
                found = jnp.int32(0)
                for k in range(slots):
                    found = listed(k, found)
            else:
                found = lax.fori_loop(0, slots, listed, jnp.int32(0))
            reach[r, b] = found.astype(jnp.float32)

    mine = trans_ref[:, pl.ds(pl.multiple_of(h * states, TILE), states)]
    low = jnp.bitwise_and(mine, TILE - 1)
    high = jnp.right_shift(mine, TILE.bit_length() - 1)
    for c in range(chunks):
        part = slice(c * width, (c + 1) * width)
        row_ids = lax.broadcasted_iota(jnp.int32, (TILE, width), 0)
        onehot[c] = jnp.where(row_ids == low[:, part], 1.0, 0.0).astype(jnp.bfloat16)

    for copy in st_copies:
        copy.wait_recv()

    total_tiles = n_st * tiles
    for c in range(chunks):
        part = slice(c * width, (c + 1) * width)
        table = raw_top[...].reshape(total_tiles, TILE).astype(jnp.bfloat16)
        picked = jnp.dot(table, onehot[c], preferred_element_type=jnp.float32)
        tile_ids = lax.broadcasted_iota(jnp.int32, (total_tiles, width), 0)
        tops[p, c] = jnp.sum(
            jnp.where(tile_ids == high[:, part], picked, 0.0), axis=0, keepdims=True)
    t_copies = []
    for d in range(1, n_dst):
        t_copies.append(remote(
            tops.at[p], tops.at[p], t_send.at[d - 1], t_recv.at[d - 1],
            dst=lax.rem(p + d, n_dst)))
        t_copies[-1].start()

    def gather(c):
        part = slice(c * width, (c + 1) * width)
        table = raw[...].reshape(total_tiles * rows, TILE)
        picked = jnp.dot(table, onehot[c], preferred_element_type=jnp.float32)
        total = picked[:rows]
        for t in range(1, total_tiles):
            total = jnp.where(high[:, part] == t, picked[t * rows:(t + 1) * rows], total)
        wbuf[p, c] = total.astype(jnp.bfloat16)

    def upward(b, c):
        return remote(wbuf.at[b, c], wbuf.at[b, c], up_send.at[b, c], w_recv.at[b, c],
                      dst=lax.rem(p + 1, n_dst))

    def downward(b, c):
        return remote(wbuf.at[b, c], wbuf.at[b, c], dn_send.at[b, c], w_recv.at[b, c],
                      dst=lax.rem(p + n_dst - 1, n_dst))

    not_last, not_first = p < n_dst - 1, p > 0

    def send_own(c):
        @pl.when(not_last)
        def _():
            upward(p, c).start()

        @pl.when(not_first)
        def _():
            downward(p, c).start()

    def relay(d, c):
        @pl.when(p >= d)
        def _():
            upward(p - d, c).wait_recv()

        @pl.when((p >= d) & not_last)
        def _():
            upward(p - d, c).start()

        @pl.when(p + d < n_dst)
        def _():
            downward(p + d, c).wait_recv()

        @pl.when((p + d < n_dst) & not_first)
        def _():
            downward(p + d, c).start()

    x_copies = {}

    def products(c):
        sums = [None] * n_org
        for r in range(n_org):
            shifted = [tops[b, c] + (reach[r, b] - 1.0) * -FLOOR for b in range(n_dst)]
            ceiling = functools.reduce(jnp.maximum, shifted)
            total = None
            for b in range(n_dst):
                scale = reach[r, b] * jnp.exp(shifted[b] - ceiling)
                term = scale * jnp.dot(
                    kern_in[b, r], wbuf[b, c], preferred_element_type=jnp.float32)
                total = term if total is None else total + term
            sums[r] = total
            if r == 0:
                own_sum[c] = total
                own_top[c] = ceiling
            else:
                x_out[r - 1, c] = total.astype(jnp.bfloat16)
                x_out_top[r - 1, c] = ceiling
                to = lax.rem(q + r, n_org)
                for i, (src, dst) in enumerate(((x_out_top, x_in_top), (x_out, x_in))):
                    copy = remote(src.at[r - 1, c], dst.at[r - 1, c],
                                  x_send.at[r - 1, c, i], x_recv.at[r - 1, c, i], org=to)
                    copy.start()
                    x_copies.setdefault(c, []).append(copy)

    def finish(c):
        for copy in x_copies.get(c, []):
            copy.wait_recv()
        ceiling = own_top[c]
        for r in range(1, n_org):
            ceiling = jnp.maximum(ceiling, x_in_top[r - 1, c])
        merged = jnp.exp(own_top[c] - ceiling) * own_sum[c]
        for r in range(1, n_org):
            merged += jnp.exp(x_in_top[r - 1, c] - ceiling) * x_in[r - 1, c].astype(jnp.float32)
        out_ref[:, c * width:(c + 1) * width] = DISCOUNT * (ceiling + jnp.log(merged))

    for c in range(min(AHEAD, chunks)):
        gather(c)
        send_own(c)
    for c in range(AHEAD, chunks):
        gather(c)
    for copy in k_copies:
        copy.wait_recv()
    for copy in t_copies:
        copy.wait_recv()
    for c in range(chunks):
        for d in range(1, n_dst):
            relay(d, c)
            if d == 1 and c + AHEAD < chunks:
                send_own(c + AHEAD)
        products(c)
        if c > 0:
            finish(c - 1)
    finish(chunks - 1)

    for copy in st_copies + k_copies + t_copies:
        copy.wait_send()
    for c in range(chunks):
        for d in range(n_dst):
            @pl.when((p >= d) & not_last)
            def _(d=d, c=c):
                upward(p - d, c).wait_send()

            @pl.when((p + d < n_dst) & not_first)
            def _(d=d, c=c):
                downward(p + d, c).wait_send()

        for copy in x_copies.get(c, []):
            copy.wait_send()


def on_device(sizes, value_now, utility, move_costs, dest_blocks, row_counts, transition):
    n_dst, n_org, n_st = sizes
    rows, states = value_now.shape[2:]
    width = min(CHUNK, states)
    chunks = states // width
    tiles = states // TILE
    peers = n_dst * n_org - 1
    others = max(n_org - 1, 1)
    vmem = pl.BlockSpec(memory_space=pltpu.VMEM)
    smem = pl.BlockSpec(memory_space=pltpu.SMEM)
    dma = pltpu.SemaphoreType.DMA
    bf16, f32 = jnp.bfloat16, jnp.float32
    partial = pl.pallas_call(
        functools.partial(sweep, sizes),
        out_shape=jax.ShapeDtypeStruct((rows, states), f32),
        in_specs=[vmem, vmem, vmem, smem, smem],
        out_specs=vmem,
        scratch_shapes=[
            pltpu.VMEM((n_st, tiles, rows, TILE), bf16),
            pltpu.VMEM((n_st, tiles, TILE), f32),
            pltpu.VMEM((n_dst, n_org, rows, rows), bf16),
            pltpu.VMEM((n_dst, n_org, rows, rows), bf16),
            pltpu.VMEM((chunks, TILE, width), bf16),
            pltpu.VMEM((n_dst, chunks, rows, width), bf16),
            pltpu.VMEM((n_dst, chunks, 1, width), f32),
            pltpu.VMEM((chunks, rows, width), f32),
            pltpu.VMEM((chunks, 1, width), f32),
            pltpu.VMEM((others, chunks, rows, width), bf16),
            pltpu.VMEM((others, chunks, 1, width), f32),
            pltpu.VMEM((others, chunks, rows, width), bf16),
            pltpu.VMEM((others, chunks, 1, width), f32),
            pltpu.SMEM((n_org, n_dst), f32),
            dma((max(n_st - 1, 1), 2)), dma((max(n_st - 1, 1), 2)),
            dma((max(peers, 1),)), dma((max(peers, 1),)),
            dma((max(n_dst - 1, 1),)), dma((max(n_dst - 1, 1),)),
            dma((n_dst, chunks)), dma((n_dst, chunks)), dma((n_dst, chunks)),
            dma((others, chunks, 2)), dma((others, chunks, 2)),
        ],
        compiler_params=pltpu.CompilerParams(
            collective_id=0, has_side_effects=True, vmem_limit_bytes=48 * 2**20
        ),
    )(
        value_now.reshape(rows, states),
        move_costs.reshape(n_dst, rows, n_org * rows),
        transition.reshape(1, -1),
        dest_blocks,
        row_counts,
    )
    return utility + partial[None, None]


def solution(mesh):
    sizes = tuple(mesh.shape[axis] for axis in ("dst", "org", "st"))
    return jax.shard_map(
        functools.partial(on_device, sizes),
        mesh=mesh,
        in_specs=(
            P(("draws", "dst"), "org", None, "st"),
            P(("draws", "dst"), "org", None, "st"),
            P("draws", "org", None, "dst", None),
            P(),
            P(),
            P(),
        ),
        out_specs=P(("draws", "dst"), "org", None, "st"),
        check_vma=False,
    )
```

time: 112 us -> 40.6 us (0.36)
  blocking collectives: 37.6 us -> 0 us
  Pallas kernels: 0 us -> 35.5 us
  waiting for transfers between devices: 32.4 us -> 0 us
  between operations: 13.6 us -> 0.02 us
  matrix products: 8.98 us -> 0 us
  local copies, waits for them, and re-layouts: 12.5 us -> 4 us
  starting transfers between devices: 3.69 us -> 0 us
  other arithmetic: 2.52 us -> 0.85 us
    pmax x1 -> x0, blocking collectives: 37.6 us -> none  [on_device(): lax.pmax(offered.astype(jnp.bfloat16), ('dst', 'org')).astype(offered.dtype)]
    pallas_call x0 -> x1, Pallas kernels: none -> 35.5 us  [on_device(): pl.pallas_call(functools.partial(sweep, sizes), out_shape=jax.ShapeDtypeS...]
    all_to_all x1 -> x0, waiting for transfers between devices: 19.7 us -> none  [on_device(): lax.all_to_all(rounded, 'dst', split_axis=0, concat_axis=0, tiled=True)]
    all_gather x2 -> x0, waiting for transfers between devices: 12.6 us -> none  [the longest x1 12.6 us: on_device(): every_state = lax.all_gather(value_now, 'st', axis=3, tiled=True)]
    dot_general x4 -> x0, matrix products: 8.98 us -> none  [dense_anchor(): return jnp.dot(kernel_row, weights, preferred_element_type=jnp.float32)]
    gather x1 -> x0, local copies, waits for them, and re-layouts: 7.05 us -> none  [on_device(): shifted = jnp.take(every_state, chosen, axis=3)]
    all_to_all x1 -> x0, starting transfers between devices: 3.65 us -> none  [on_device(): lax.all_to_all(rounded, 'dst', split_axis=0, concat_axis=0, tiled=True)]
    unnamed x13, local copies, waits for them, and re-layouts: 2.52 us -> 4 us
  transfers between devices with their start and end apart: 3 -> 0, of which waited for: 2 -> 0; matrix products, arithmetic and copies ran while one was open for 1% -> 0% of each run, Pallas kernels for 0% -> 0%
where the time goes in v1:
time: 40.6 us; the launch traced here: 40.4 us
  Pallas kernels  35.5 us (87%)
  local copies, waits for them, and re-layouts  4 us (10%)
  other arithmetic  0.85 us (2%)
    pallas_call x1, Pallas kernels, on_device(): pl.pallas_call(functools.partial(sweep, sizes), out_shape=jax.ShapeDtypeS...  35.5 us
    unnamed x13, local copies, waits for them, and re-layouts  4 us
    add x1, other arithmetic, on_device(): return utility + partial[None, None]  0.85 us

profile of v1, /device:TPU:0, one launch (start us, length us, event | category | flops | bytes accessed | tf_op | source)
XLA Modules:
  0.0 40.4 jit_solution(14567602427448790158)
XLA Ops:
  0.0 0.0 copy-start.5
  0.0 0.7 %copy-done.5 = s32[8,3]{0,1:T(4,128)S(1)} copy-done((s32[8,3]{0,1:T(4,128)S(1)}, s32[8,3]{0,1:T(4,128)}, u32[]{:S(2)}) %copy-start.5) | copy-done | bytes 120
  0.7 0.0 copy-start.3
  0.7 0.1 copy.7.lists_ref
  0.8 0.6 %copy-done.3 = s32[8]{0:T(128)S(1)} copy-done((s32[8]{0:T(128)S(1)}, s32[8]{0:T(128)}, u32[]{:S(2)}) %copy-start.3) | copy-done | bytes 56
  1.3 0.0 copy-start
  1.3 1.0 %copy-done = f32[1,1,64,2048]{3,2,1,0:T(8,128)S(1)} copy-done((f32[1,1,64,2048]{3,2,1,0:T(8,128)S(1)}, f32[1,1,64,2048]{3,2,1,0:T(8,128)}, u32[]{:S(2)}) %copy-start) | copy-done | bytes 524312
  2.4 0.0 copy-start.1
  2.4 0.9 %copy-done.1 = f32[4,1,64,1,128]{4,3,2,1,0:T(1,128)S(1)} copy-done((f32[4,1,64,1,128]{4,3,2,1,0:T(1,128)S(1)}, f32[4,1,64,1,128]{4,3,2,1,0:T(1,128)}, u32[]{:S(2)}) %copy-start.1) | copy-done | bytes 131096
  3.3 0.0 copy-start.2
  3.3 0.7 %copy-done.2 = s32[4096]{0:T(1024)S(1)} copy-done((s32[4096]{0:T(1024)S(1)}, s32[4096]{0:T(1024)}, u32[]{:S(2)}) %copy-start.2) | copy-done | bytes 16408
  4.0 0.0 copy-start.4
  4.0 35.5 %shard_map.64 = f32[64,2048]{1,0:T(8,128)S(1)} custom-call(f32[64,2048]{1,0:T(8,128)S(1)} %bitcast.5, f32[4,64,128]{2,1,0:T(8,128)S(1)} %bitcast.6, s32[1,4096]{1,0:T(1,128)S(1)} %bitcast.7, s32[8,3]{1,0:T(8,128)S(1)} %copy.7.lists_ref, s32[8]{0:T(128)S(1)} %copy-done.3), custom_call_target="tpu_custom_call" | custom-call | tf_op jit(solution)/shard_map/pallas_call | solution.py:254
  39.5 0.0 copy-done.4
  39.5 0.9 %bitcast_add_fusion = f32[1,1,64,2048]{3,2,1,0:T(8,128)} fusion(f32[1,1,64,2048]{3,2,1,0:T(8,128)S(1)} %copy-done.4, f32[64,2048]{1,0:T(8,128)S(1)} %shard_map.64), kind=kLoop, calls=%fused_computation | loop fusion | flops 131072 | bytes 1572864 | tf_op jit(solution)/shard_map/add | solution.py:290
Async XLA Ops:
  0.0 0.7 %copy-start.5 = (s32[8,3]{0,1:T(4,128)S(1)}, s32[8,3]{0,1:T(4,128)}, u32[]{:S(2)}) copy-start(s32[8,3]{0,1:T(4,128)} %param.9) | copy-start | bytes 292
  0.7 0.7 %copy-start.3 = (s32[8]{0:T(128)S(1)}, s32[8]{0:T(128)}, u32[]{:S(2)}) copy-start(s32[8]{0:T(128)} %counts_ref.1) | copy-start | bytes 100
  1.3 1.0 %copy-start = (f32[1,1,64,2048]{3,2,1,0:T(8,128)S(1)}, f32[1,1,64,2048]{3,2,1,0:T(8,128)}, u32[]{:S(2)}) copy-start(f32[1,1,64,2048]{3,2,1,0:T(8,128)} %param.6) | copy-start | bytes 1572868
  2.4 0.9 %copy-start.1 = (f32[4,1,64,1,128]{4,3,2,1,0:T(1,128)S(1)}, f32[4,1,64,1,128]{4,3,2,1,0:T(1,128)}, u32[]{:S(2)}) copy-start(f32[4,1,64,1,128]{4,3,2,1,0:T(1,128)} %param.8) | copy-start | bytes 393220
  3.3 0.7 %copy-start.2 = (s32[4096]{0:T(1024)S(1)}, s32[4096]{0:T(1024)}, u32[]{:S(2)}) copy-start(s32[4096]{0:T(1024)} %param.11) | copy-start | bytes 49156
  4.0 35.5 %copy-start.4 = (f32[1,1,64,2048]{3,2,1,0:T(8,128)S(1)}, f32[1,1,64,2048]{3,2,1,0:T(8,128)}, u32[]{:S(2)}) copy-start(f32[1,1,64,2048]{3,2,1,0:T(8,128)} %param.7) | copy-start | bytes 1572868

commit v2 on v1

--- a/solution.py
+++ b/solution.py
@@ -16,7 +16,8 @@
 
 
 def sweep(
-    sizes, v_ref, cost_ref, trans_ref, lists_ref, counts_ref, out_ref,
+    sizes, v_in, cost_in, trans_in, lists_in, counts_in, out_ref,
+    v_ref, cost_ref, trans_ref, lists_ref, counts_ref, in_sem,
     raw, raw_top, kern_out, kern_in, onehot, wbuf, tops, own_sum, own_top,
     x_out, x_out_top, x_in, x_in_top, reach,
     st_send, st_recv, k_send, k_recv, t_send, t_recv, up_send, dn_send, w_recv, x_send, x_recv,
@@ -25,7 +26,7 @@
     rows, states = v_ref.shape
     tiles = states // TILE
     chunks, width = wbuf.shape[1], wbuf.shape[3]
-    slots = lists_ref.shape[1]
+    slots = lists_ref.shape[0]
     p = lax.axis_index("dst")
     q = lax.axis_index("org")
     h = lax.axis_index("st")
@@ -36,6 +37,14 @@
             device_id=where, device_id_type=MESH,
         )
 
+    fetches = [
+        pltpu.make_async_copy(source, target, in_sem.at[i])
+        for i, (source, target) in enumerate((
+            (v_in, v_ref), (cost_in, cost_ref), (trans_in, trans_ref),
+            (lists_in, lists_ref), (counts_in, counts_ref)))
+    ]
+    for fetch in fetches:
+        fetch.start()
     peers = [(a, b) for a in range(n_dst) for b in range(n_org) if (a, b) != (0, 0)]
     barrier = pltpu.get_barrier_semaphore()
     for dp, dq in peers:
@@ -48,6 +57,7 @@
             barrier, inc=1, device_id_type=MESH, device_id={"st": lax.rem(h + d, n_st)}
         )
 
+    fetches[0].wait()
     for t in range(tiles):
         x = v_ref[:, t * TILE:(t + 1) * TILE]
         top = jnp.max(x, axis=0, keepdims=True).astype(jnp.bfloat16).astype(jnp.float32)
@@ -64,6 +74,8 @@
                 buf.at[h], buf.at[h], st_send.at[d - 1, i], st_recv.at[d - 1, i], st=other))
             st_copies[-1].start()
 
+    for fetch in fetches[1:]:
+        fetch.wait()
     for a in range(n_dst):
         k = jnp.exp(-cost_ref[a]).astype(jnp.bfloat16)
         for b in range(n_org):
@@ -84,7 +96,7 @@
             block = b * n_org + q
 
             def listed(k, found, anchor=anchor, block=block, count=count):
-                hit = jnp.where(lists_ref[anchor, k] == block, 1, 0)
+                hit = jnp.where(lists_ref[k, anchor] == block, 1, 0)
                 return found + hit * jnp.where(k < count, 1, 0)
 
             if slots <= 4:
@@ -213,14 +225,18 @@
         copy.wait_recv()
     for copy in t_copies:
         copy.wait_recv()
-    for c in range(chunks):
+    for wave in range(chunks + n_dst - 2):
         for d in range(1, n_dst):
-            relay(d, c)
-            if d == 1 and c + AHEAD < chunks:
-                send_own(c + AHEAD)
-        products(c)
-        if c > 0:
-            finish(c - 1)
+            c = wave - d + 1
+            if 0 <= c < chunks:
+                relay(d, c)
+                if d == 1 and c + AHEAD < chunks:
+                    send_own(c + AHEAD)
+        done = wave - n_dst + 2
+        if done >= 0:
+            products(done)
+        if done >= 1:
+            finish(done - 1)
     finish(chunks - 1)
 
     for copy in st_copies + k_copies + t_copies:
@@ -248,15 +264,21 @@
     peers = n_dst * n_org - 1
     others = max(n_org - 1, 1)
     vmem = pl.BlockSpec(memory_space=pltpu.VMEM)
-    smem = pl.BlockSpec(memory_space=pltpu.SMEM)
+    hbm = pl.BlockSpec(memory_space=pltpu.HBM)
     dma = pltpu.SemaphoreType.DMA
     bf16, f32 = jnp.bfloat16, jnp.float32
     partial = pl.pallas_call(
         functools.partial(sweep, sizes),
         out_shape=jax.ShapeDtypeStruct((rows, states), f32),
-        in_specs=[vmem, vmem, vmem, smem, smem],
+        in_specs=[hbm] * 5,
         out_specs=vmem,
         scratch_shapes=[
+            pltpu.VMEM((rows, states), f32),
+            pltpu.VMEM((n_dst, rows, n_org * rows), f32),
+            pltpu.VMEM((1, transition.shape[0]), jnp.int32),
+            pltpu.SMEM(dest_blocks.shape[::-1], jnp.int32),
+            pltpu.SMEM(row_counts.shape, jnp.int32),
+            dma((5,)),
             pltpu.VMEM((n_st, tiles, rows, TILE), bf16),
             pltpu.VMEM((n_st, tiles, TILE), f32),
             pltpu.VMEM((n_dst, n_org, rows, rows), bf16),
@@ -278,13 +300,13 @@
             dma((others, chunks, 2)), dma((others, chunks, 2)),
         ],
         compiler_params=pltpu.CompilerParams(
-            collective_id=0, has_side_effects=True, vmem_limit_bytes=48 * 2**20
+            collective_id=0, has_side_effects=True, vmem_limit_bytes=63 * 2**20
         ),
     )(
         value_now.reshape(rows, states),
         move_costs.reshape(n_dst, rows, n_org * rows),
         transition.reshape(1, -1),
-        dest_blocks,
+        dest_blocks.T,
         row_counts,
     )
     return utility + partial[None, None]

time: 40.6 us -> 35.8 us (0.88)
  local copies, waits for them, and re-layouts: 4 us -> 0.01 us
  Pallas kernels: 35.5 us -> 33.7 us
  other arithmetic: 0.85 us -> 1.89 us
    unnamed x13 -> x2, local copies, waits for them, and re-layouts: 4 us -> 0.01 us
    pallas_call x1, Pallas kernels: 35.5 us -> 33.7 us  [on_device(): pl.pallas_call(functools.partial(sweep, sizes), out_shape=jax.ShapeDtypeS...]
    add x1, other arithmetic: 0.85 us -> 1.89 us  [on_device(): return utility + partial[None, None]]
where the time goes in v2:
time: 35.8 us; the launch traced here: 35.6 us
  Pallas kernels  33.7 us (94%)
  other arithmetic  1.89 us (5%)
    pallas_call x1, Pallas kernels, on_device(): pl.pallas_call(functools.partial(sweep, sizes), out_shape=jax.ShapeDtypeS...  33.7 us
    add x1, other arithmetic, on_device(): return utility + partial[None, None]  1.89 us

profile of v2, /device:TPU:0, one launch (start us, length us, event | category | flops | bytes accessed | tf_op | source)
XLA Modules:
  0.0 35.6 jit_solution(4223540059891658655)
XLA Ops:
  0.0 0.0 copy-start
  0.0 33.7 %shard_map.64 = f32[64,2048]{1,0:T(8,128)} custom-call(f32[64,2048]{1,0:T(8,128)} %bitcast.6, f32[4,64,128]{2,1,0:T(8,128)} %bitcast.7, s32[1,4096]{1,0:T(1,128)} %bitcast.8, s32[3,8]{1,0:T(4,128)} %bitcast.9, s32[8]{0:T(128)} %counts_in.1), custom_call_target="tpu_custom_call" | custom-call | tf_op jit(solution)/shard_map/pallas_call | solution.py:270
  33.7 0.0 copy-done
  33.7 1.9 %bitcast_add_fusion = f32[1,1,64,2048]{3,2,1,0:T(8,128)} fusion(f32[1,1,64,2048]{3,2,1,0:T(8,128)S(1)} %copy-done, f32[64,2048]{1,0:T(8,128)} %shard_map.64), kind=kLoop, calls=%fused_computation | loop fusion | flops 131072 | bytes 1572864 | tf_op jit(solution)/shard_map/add | solution.py:312
Async XLA Ops:
  0.0 33.7 %copy-start = (f32[1,1,64,2048]{3,2,1,0:T(8,128)S(1)}, f32[1,1,64,2048]{3,2,1,0:T(8,128)}, u32[]{:S(2)}) copy-start(f32[1,1,64,2048]{3,2,1,0:T(8,128)} %param.7) | copy-start | bytes 1572868

commit v3 on v2

--- a/solution.py
+++ b/solution.py
@@ -10,8 +10,8 @@
 DISCOUNT = 0.95
 FLOOR = -1e30
 TILE = 256
-CHUNK = 512
-AHEAD = 2
+CHUNK = 256
+AHEAD = 3
 MESH = pl.DeviceIdType.MESH
 
 
@@ -19,8 +19,9 @@
     sizes, v_in, cost_in, trans_in, lists_in, counts_in, out_ref,
     v_ref, cost_ref, trans_ref, lists_ref, counts_ref, in_sem,
     raw, raw_top, kern_out, kern_in, onehot, wbuf, tops, own_sum, own_top,
-    x_out, x_out_top, x_in, x_in_top, reach,
+    x_out, x_out_top, x_in, x_in_top, z_out, z_out_top, z_in, z_in_top, reach,
     st_send, st_recv, k_send, k_recv, t_send, t_recv, up_send, dn_send, w_recv, x_send, x_recv,
+    z_send, z_recv,
 ):
     n_dst, n_org, n_st = sizes
     rows, states = v_ref.shape
@@ -30,6 +31,11 @@
     p = lax.axis_index("dst")
     q = lax.axis_index("org")
     h = lax.axis_index("st")
+    last = n_dst - 1
+    inner = (p > 0) & (p < last)
+    server = (p == 1) | (p == last - 1)
+    served = jnp.where(p == 1, 0, last)
+    active = (inner, server)
 
     def remote(source, target, send, recv, **where):
         return pltpu.make_async_remote_copy(
@@ -80,17 +86,40 @@
         k = jnp.exp(-cost_ref[a]).astype(jnp.bfloat16)
         for b in range(n_org):
             kern_out[a, b] = k[:, b * rows:(b + 1) * rows]
-    k_copies = []
-    for i, (dp, dq) in enumerate(peers):
-        to_p, to_q = lax.rem(p + dp, n_dst), lax.rem(q + dq, n_org)
-        k_copies.append(remote(
-            kern_out.at[to_p, to_q], kern_in.at[p, (n_org - dq) % n_org],
-            k_send.at[i], k_recv.at[i], dst=to_p, org=to_q))
-        k_copies[-1].start()
-    kern_in[p, 0] = kern_out[p, q]
-
-    for r in range(n_org):
-        anchor = p * n_org + lax.rem(q + r, n_org)
+
+    def cost_copy(a, dq):
+        target = min(max(a, 1), last - 1)
+        return remote(
+            kern_out.at[a, lax.rem(q + dq, n_org)],
+            kern_in.at[int(a != target), p, (n_org - dq) % n_org],
+            k_send.at[a, dq], k_recv.at[int(a != target), p, (n_org - dq) % n_org],
+            dst=target, org=lax.rem(q + dq, n_org))
+
+    for a in range(n_dst):
+        target = min(max(a, 1), last - 1)
+        for dq in range(1, n_org):
+            cost_copy(a, dq).start()
+
+        @pl.when(p != target)
+        def _(a=a):
+            cost_copy(a, 0).start()
+
+        @pl.when(p == target)
+        def _(a=a, target=target):
+            kern_in[int(a != target), p, 0] = kern_out[a, q]
+
+    def cost_arrivals():
+        for slot in range(2):
+            for b in range(n_dst):
+                for r in range(n_org):
+                    @pl.when(active[slot] if r else active[slot] & (p != b))
+                    def _(slot=slot, b=b, r=r):
+                        place = kern_in.at[slot, b, r]
+                        remote(place, place, k_send.at[0, 0], k_recv.at[slot, b, r],
+                               dst=lax.rem(p + 1, n_dst)).wait_recv()
+
+    for slot, r in ((i, j) for i in range(2) for j in range(n_org)):
+        anchor = (served if slot else p) * n_org + lax.rem(q + r, n_org)
         count = counts_ref[anchor]
         for b in range(n_dst):
             block = b * n_org + q
@@ -105,7 +134,7 @@
                     found = listed(k, found)
             else:
                 found = lax.fori_loop(0, slots, listed, jnp.int32(0))
-            reach[r, b] = found.astype(jnp.float32)
+            reach[slot, r, b] = found.astype(jnp.float32)
 
     mine = trans_ref[:, pl.ds(pl.multiple_of(h * states, TILE), states)]
     low = jnp.bitwise_and(mine, TILE - 1)
@@ -150,109 +179,148 @@
         return remote(wbuf.at[b, c], wbuf.at[b, c], dn_send.at[b, c], w_recv.at[b, c],
                       dst=lax.rem(p + n_dst - 1, n_dst))
 
-    not_last, not_first = p < n_dst - 1, p > 0
+    can_up, can_down = p < last - 1, p > 1
 
     def send_own(c):
-        @pl.when(not_last)
+        @pl.when(can_up)
         def _():
             upward(p, c).start()
 
-        @pl.when(not_first)
+        @pl.when(can_down)
         def _():
             downward(p, c).start()
 
     def relay(d, c):
-        @pl.when(p >= d)
+        @pl.when((p >= d) & inner)
         def _():
             upward(p - d, c).wait_recv()
 
-        @pl.when((p >= d) & not_last)
+        @pl.when((p >= d) & can_up)
         def _():
             upward(p - d, c).start()
 
-        @pl.when(p + d < n_dst)
+        @pl.when((p + d < n_dst) & inner)
         def _():
             downward(p + d, c).wait_recv()
 
-        @pl.when((p + d < n_dst) & not_first)
+        @pl.when((p + d < n_dst) & can_down)
         def _():
             downward(p + d, c).start()
 
-    x_copies = {}
-
-    def products(c):
-        sums = [None] * n_org
-        for r in range(n_org):
-            shifted = [tops[b, c] + (reach[r, b] - 1.0) * -FLOOR for b in range(n_dst)]
+    def across(slot, r, c):
+        at = (slot, r - 1, c)
+        return [
+            remote(source.at[at], target.at[at], x_send.at[slot, r - 1, c, i],
+                   x_recv.at[slot, r - 1, c, i], org=lax.rem(q + r, n_org))
+            for i, (source, target) in enumerate(((x_out_top, x_in_top), (x_out, x_in)))
+        ]
+
+    def outward(c):
+        return [
+            remote(source.at[c], target.at[c], z_send.at[c, i], z_recv.at[c, i], dst=served)
+            for i, (source, target) in enumerate(((z_out_top, z_in_top), (z_out, z_in)))
+        ]
+
+    def products(slot, c):
+        for r in reversed(range(n_org)):
+            shifted = [tops[b, c] + (reach[slot, r, b] - 1.0) * -FLOOR for b in range(n_dst)]
             ceiling = functools.reduce(jnp.maximum, shifted)
             total = None
             for b in range(n_dst):
-                scale = reach[r, b] * jnp.exp(shifted[b] - ceiling)
+                scale = reach[slot, r, b] * jnp.exp(shifted[b] - ceiling)
                 term = scale * jnp.dot(
-                    kern_in[b, r], wbuf[b, c], preferred_element_type=jnp.float32)
+                    kern_in[slot, b, r], wbuf[b, c], preferred_element_type=jnp.float32)
                 total = term if total is None else total + term
-            sums[r] = total
             if r == 0:
-                own_sum[c] = total
-                own_top[c] = ceiling
+                own_sum[slot, c] = total
+                own_top[slot, c] = ceiling
             else:
-                x_out[r - 1, c] = total.astype(jnp.bfloat16)
-                x_out_top[r - 1, c] = ceiling
-                to = lax.rem(q + r, n_org)
-                for i, (src, dst) in enumerate(((x_out_top, x_in_top), (x_out, x_in))):
-                    copy = remote(src.at[r - 1, c], dst.at[r - 1, c],
-                                  x_send.at[r - 1, c, i], x_recv.at[r - 1, c, i], org=to)
+                x_out[slot, r - 1, c] = total.astype(jnp.bfloat16)
+                x_out_top[slot, r - 1, c] = ceiling
+                for copy in across(slot, r, c):
                     copy.start()
-                    x_copies.setdefault(c, []).append(copy)
-
-    def finish(c):
-        for copy in x_copies.get(c, []):
-            copy.wait_recv()
-        ceiling = own_top[c]
+
+    def finish(slot, c):
         for r in range(1, n_org):
-            ceiling = jnp.maximum(ceiling, x_in_top[r - 1, c])
-        merged = jnp.exp(own_top[c] - ceiling) * own_sum[c]
+            for copy in across(slot, r, c):
+                copy.wait_recv()
+        ceiling = own_top[slot, c]
         for r in range(1, n_org):
-            merged += jnp.exp(x_in_top[r - 1, c] - ceiling) * x_in[r - 1, c].astype(jnp.float32)
-        out_ref[:, c * width:(c + 1) * width] = DISCOUNT * (ceiling + jnp.log(merged))
+            ceiling = jnp.maximum(ceiling, x_in_top[slot, r - 1, c])
+        merged = jnp.exp(own_top[slot, c] - ceiling) * own_sum[slot, c]
+        for r in range(1, n_org):
+            merged += (jnp.exp(x_in_top[slot, r - 1, c] - ceiling)
+                       * x_in[slot, r - 1, c].astype(jnp.float32))
+        if slot:
+            z_out[c] = merged.astype(jnp.bfloat16)
+            z_out_top[c] = ceiling
+            for copy in outward(c):
+                copy.start()
+        else:
+            out_ref[:, c * width:(c + 1) * width] = DISCOUNT * (ceiling + jnp.log(merged))
+
+    def both(step, c):
+        for slot in (1, 0):
+            @pl.when(active[slot])
+            def _(slot=slot):
+                step(slot, c)
 
     for c in range(min(AHEAD, chunks)):
         gather(c)
         send_own(c)
     for c in range(AHEAD, chunks):
         gather(c)
-    for copy in k_copies:
-        copy.wait_recv()
+    cost_arrivals()
     for copy in t_copies:
         copy.wait_recv()
-    for wave in range(chunks + n_dst - 2):
-        for d in range(1, n_dst):
+    for wave in range(chunks + n_dst - 3):
+        for d in range(1, n_dst - 1):
             c = wave - d + 1
             if 0 <= c < chunks:
                 relay(d, c)
                 if d == 1 and c + AHEAD < chunks:
                     send_own(c + AHEAD)
-        done = wave - n_dst + 2
+        done = wave - n_dst + 3
         if done >= 0:
-            products(done)
+            both(products, done)
         if done >= 1:
-            finish(done - 1)
-    finish(chunks - 1)
-
-    for copy in st_copies + k_copies + t_copies:
+            both(finish, done - 1)
+    both(finish, chunks - 1)
+
+    @pl.when(jnp.logical_not(inner))
+    def _():
+        for c in range(chunks):
+            for copy in outward(c):
+                copy.wait_recv()
+            out_ref[:, c * width:(c + 1) * width] = DISCOUNT * (
+                z_in_top[c] + jnp.log(z_in[c].astype(jnp.float32)))
+
+    for copy in st_copies + t_copies:
         copy.wait_send()
+    for a in range(n_dst):
+        for dq in range(1, n_org):
+            cost_copy(a, dq).wait_send()
+
+        @pl.when(p != min(max(a, 1), last - 1))
+        def _(a=a):
+            cost_copy(a, 0).wait_send()
+
     for c in range(chunks):
         for d in range(n_dst):
-            @pl.when((p >= d) & not_last)
+            @pl.when((p >= d) & can_up)
             def _(d=d, c=c):
                 upward(p - d, c).wait_send()
 
-            @pl.when((p + d < n_dst) & not_first)
+            @pl.when((p + d < n_dst) & can_down)
             def _(d=d, c=c):
                 downward(p + d, c).wait_send()
 
-        for copy in x_copies.get(c, []):
-            copy.wait_send()
+        for slot in range(2):
+            @pl.when(active[slot])
+            def _(slot=slot, c=c):
+                copies = [copy for r in range(1, n_org) for copy in across(slot, r, c)]
+                for copy in copies + (outward(c) if slot else []):
+                    copy.wait_send()
 
 
 def on_device(sizes, value_now, utility, move_costs, dest_blocks, row_counts, transition):
@@ -261,7 +329,6 @@
     width = min(CHUNK, states)
     chunks = states // width
     tiles = states // TILE
-    peers = n_dst * n_org - 1
     others = max(n_org - 1, 1)
     vmem = pl.BlockSpec(memory_space=pltpu.VMEM)
     hbm = pl.BlockSpec(memory_space=pltpu.HBM)
@@ -282,22 +349,27 @@
             pltpu.VMEM((n_st, tiles, rows, TILE), bf16),
             pltpu.VMEM((n_st, tiles, TILE), f32),
             pltpu.VMEM((n_dst, n_org, rows, rows), bf16),
-            pltpu.VMEM((n_dst, n_org, rows, rows), bf16),
+            pltpu.VMEM((2, n_dst, n_org, rows, rows), bf16),
             pltpu.VMEM((chunks, TILE, width), bf16),
             pltpu.VMEM((n_dst, chunks, rows, width), bf16),
             pltpu.VMEM((n_dst, chunks, 1, width), f32),
-            pltpu.VMEM((chunks, rows, width), f32),
+            pltpu.VMEM((2, chunks, rows, width), f32),
+            pltpu.VMEM((2, chunks, 1, width), f32),
+            pltpu.VMEM((2, others, chunks, rows, width), bf16),
+            pltpu.VMEM((2, others, chunks, 1, width), f32),
+            pltpu.VMEM((2, others, chunks, rows, width), bf16),
+            pltpu.VMEM((2, others, chunks, 1, width), f32),
+            pltpu.VMEM((chunks, rows, width), bf16),
             pltpu.VMEM((chunks, 1, width), f32),
-            pltpu.VMEM((others, chunks, rows, width), bf16),
-            pltpu.VMEM((others, chunks, 1, width), f32),
-            pltpu.VMEM((others, chunks, rows, width), bf16),
-            pltpu.VMEM((others, chunks, 1, width), f32),
-            pltpu.SMEM((n_org, n_dst), f32),
+            pltpu.VMEM((chunks, rows, width), bf16),
+            pltpu.VMEM((chunks, 1, width), f32),
+            pltpu.SMEM((2, n_org, n_dst), f32),
             dma((max(n_st - 1, 1), 2)), dma((max(n_st - 1, 1), 2)),
-            dma((max(peers, 1),)), dma((max(peers, 1),)),
+            dma((n_dst, n_org)), dma((2, n_dst, n_org)),
             dma((max(n_dst - 1, 1),)), dma((max(n_dst - 1, 1),)),
             dma((n_dst, chunks)), dma((n_dst, chunks)), dma((n_dst, chunks)),
-            dma((others, chunks, 2)), dma((others, chunks, 2)),
+            dma((2, others, chunks, 2)), dma((2, others, chunks, 2)),
+            dma((chunks, 2)), dma((chunks, 2)),
         ],
         compiler_params=pltpu.CompilerParams(
             collective_id=0, has_side_effects=True, vmem_limit_bytes=63 * 2**20

time: 35.8 us -> 40.6 us (1.13)
  Pallas kernels: 33.7 us -> 38.5 us
    pallas_call x1, Pallas kernels: 33.7 us -> 38.5 us  [on_device(): pl.pallas_call(functools.partial(sweep, sizes), out_shape=jax.ShapeDtypeS...]
where the time goes in v3:
time: 40.6 us; the launch traced here: 40.4 us
  Pallas kernels  38.5 us (95%)
  other arithmetic  1.89 us (5%)
    pallas_call x1, Pallas kernels, on_device(): pl.pallas_call(functools.partial(sweep, sizes), out_shape=jax.ShapeDtypeS...  38.5 us
    add x1, other arithmetic, on_device(): return utility + partial[None, None]  1.89 us

profile of v3, /device:TPU:0, one launch (start us, length us, event | category | flops | bytes accessed | tf_op | source)
XLA Modules:
  0.0 40.4 jit_solution(11229120928296799642)
XLA Ops:
  0.0 0.0 copy-start
  0.0 38.5 %shard_map.64 = f32[64,2048]{1,0:T(8,128)} custom-call(f32[64,2048]{1,0:T(8,128)} %bitcast.6, f32[4,64,128]{2,1,0:T(8,128)} %bitcast.7, s32[1,4096]{1,0:T(1,128)} %bitcast.8, s32[3,8]{1,0:T(4,128)} %bitcast.9, s32[8]{0:T(128)} %counts_in.1), custom_call_target="tpu_custom_call" | custom-call | tf_op jit(solution)/shard_map/pallas_call | solution.py:337
  38.5 0.0 copy-done
  38.6 1.9 %bitcast_add_fusion = f32[1,1,64,2048]{3,2,1,0:T(8,128)} fusion(f32[1,1,64,2048]{3,2,1,0:T(8,128)S(1)} %copy-done, f32[64,2048]{1,0:T(8,128)} %shard_map.64), kind=kLoop, calls=%fused_computation | loop fusion | flops 131072 | bytes 1572864 | tf_op jit(solution)/shard_map/add | solution.py:384
Async XLA Ops:
  0.0 38.5 %copy-start = (f32[1,1,64,2048]{3,2,1,0:T(8,128)S(1)}, f32[1,1,64,2048]{3,2,1,0:T(8,128)}, u32[]{:S(2)}) copy-start(f32[1,1,64,2048]{3,2,1,0:T(8,128)} %param.7) | copy-start | bytes 1572868

commit v4 on v3

--- a/solution.py
+++ b/solution.py
@@ -10,8 +10,8 @@
 DISCOUNT = 0.95
 FLOOR = -1e30
 TILE = 256
-CHUNK = 256
-AHEAD = 3
+CHUNK = 512
+AHEAD = 2
 MESH = pl.DeviceIdType.MESH
 
 
@@ -91,7 +91,7 @@
         target = min(max(a, 1), last - 1)
         return remote(
             kern_out.at[a, lax.rem(q + dq, n_org)],
-            kern_in.at[int(a != target), p, (n_org - dq) % n_org],
+            kern_in.at[p, int(a != target), (n_org - dq) % n_org],
             k_send.at[a, dq], k_recv.at[int(a != target), p, (n_org - dq) % n_org],
             dst=target, org=lax.rem(q + dq, n_org))
 
@@ -106,7 +106,7 @@
 
         @pl.when(p == target)
         def _(a=a, target=target):
-            kern_in[int(a != target), p, 0] = kern_out[a, q]
+            kern_in[p, int(a != target), 0] = kern_out[a, q]
 
     def cost_arrivals():
         for slot in range(2):
@@ -114,7 +114,7 @@
                 for r in range(n_org):
                     @pl.when(active[slot] if r else active[slot] & (p != b))
                     def _(slot=slot, b=b, r=r):
-                        place = kern_in.at[slot, b, r]
+                        place = kern_in.at[b, slot, r]
                         remote(place, place, k_send.at[0, 0], k_recv.at[slot, b, r],
                                dst=lax.rem(p + 1, n_dst)).wait_recv()
 
@@ -221,24 +221,36 @@
             for i, (source, target) in enumerate(((z_out_top, z_in_top), (z_out, z_in)))
         ]
 
-    def products(slot, c):
-        for r in reversed(range(n_org)):
+    anchors = [(slot, r) for slot in range(2) for r in range(n_org)]
+
+    def products(c):
+        ceilings, scales = {}, {}
+        for slot, r in anchors:
             shifted = [tops[b, c] + (reach[slot, r, b] - 1.0) * -FLOOR for b in range(n_dst)]
             ceiling = functools.reduce(jnp.maximum, shifted)
-            total = None
+            ceilings[slot, r] = ceiling
             for b in range(n_dst):
-                scale = reach[slot, r, b] * jnp.exp(shifted[b] - ceiling)
-                term = scale * jnp.dot(
-                    kern_in[slot, b, r], wbuf[b, c], preferred_element_type=jnp.float32)
-                total = term if total is None else total + term
+                scales[slot, r, b] = reach[slot, r, b] * jnp.exp(shifted[b] - ceiling)
+        totals = {}
+        for b in range(n_dst):
+            stacked = kern_in[b].reshape(len(anchors) * rows, rows)
+            product = jnp.dot(stacked, wbuf[b, c], preferred_element_type=jnp.float32)
+            for i, (slot, r) in enumerate(anchors):
+                term = scales[slot, r, b] * product[i * rows:(i + 1) * rows]
+                totals[slot, r] = totals[slot, r] + term if b else term
+        for slot, r in anchors:
             if r == 0:
-                own_sum[slot, c] = total
-                own_top[slot, c] = ceiling
+                own_sum[slot, c] = totals[slot, r]
+                own_top[slot, c] = ceilings[slot, r]
             else:
-                x_out[slot, r - 1, c] = total.astype(jnp.bfloat16)
-                x_out_top[slot, r - 1, c] = ceiling
-                for copy in across(slot, r, c):
-                    copy.start()
+                x_out[slot, r - 1, c] = totals[slot, r].astype(jnp.bfloat16)
+                x_out_top[slot, r - 1, c] = ceilings[slot, r]
+        for slot in (1, 0):
+            @pl.when(active[slot])
+            def _(slot=slot):
+                for r in range(1, n_org):
+                    for copy in across(slot, r, c):
+                        copy.start()
 
     def finish(slot, c):
         for r in range(1, n_org):
@@ -282,7 +294,9 @@
                     send_own(c + AHEAD)
         done = wave - n_dst + 3
         if done >= 0:
-            both(products, done)
+            @pl.when(inner)
+            def _(done=done):
+                products(done)
         if done >= 1:
             both(finish, done - 1)
     both(finish, chunks - 1)
@@ -349,7 +363,7 @@
             pltpu.VMEM((n_st, tiles, rows, TILE), bf16),
             pltpu.VMEM((n_st, tiles, TILE), f32),
             pltpu.VMEM((n_dst, n_org, rows, rows), bf16),
-            pltpu.VMEM((2, n_dst, n_org, rows, rows), bf16),
+            pltpu.VMEM((n_dst, 2, n_org, rows, rows), bf16),
             pltpu.VMEM((chunks, TILE, width), bf16),
             pltpu.VMEM((n_dst, chunks, rows, width), bf16),
             pltpu.VMEM((n_dst, chunks, 1, width), f32),

time: 40.6 us -> 36.5 us (0.90)
  Pallas kernels: 38.5 us -> 34.4 us
    pallas_call x1, Pallas kernels: 38.5 us -> 34.4 us  [on_device(): pl.pallas_call(functools.partial(sweep, sizes), out_shape=jax.ShapeDtypeS...]
where the time goes in v4:
time: 36.5 us; the launch traced here: 36.3 us
  Pallas kernels  34.4 us (94%)
  other arithmetic  1.89 us (5%)
    pallas_call x1, Pallas kernels, on_device(): pl.pallas_call(functools.partial(sweep, sizes), out_shape=jax.ShapeDtypeS...  34.4 us
    add x1, other arithmetic, on_device(): return utility + partial[None, None]  1.89 us

profile of v4, /device:TPU:0, one launch (start us, length us, event | category | flops | bytes accessed | tf_op | source)
XLA Modules:
  0.0 36.3 jit_solution(17410823386624169895)
XLA Ops:
  0.0 0.0 copy-start
  0.0 34.4 %shard_map.64 = f32[64,2048]{1,0:T(8,128)} custom-call(f32[64,2048]{1,0:T(8,128)} %bitcast.6, f32[4,64,128]{2,1,0:T(8,128)} %bitcast.7, s32[1,4096]{1,0:T(1,128)} %bitcast.8, s32[3,8]{1,0:T(4,128)} %bitcast.9, s32[8]{0:T(128)} %counts_in.1), custom_call_target="tpu_custom_call" | custom-call | tf_op jit(solution)/shard_map/pallas_call | solution.py:351
  34.4 0.0 copy-done
  34.4 1.9 %bitcast_add_fusion = f32[1,1,64,2048]{3,2,1,0:T(8,128)} fusion(f32[1,1,64,2048]{3,2,1,0:T(8,128)S(1)} %copy-done, f32[64,2048]{1,0:T(8,128)} %shard_map.64), kind=kLoop, calls=%fused_computation | loop fusion | flops 131072 | bytes 1572864 | tf_op jit(solution)/shard_map/add | solution.py:398
Async XLA Ops:
  0.0 34.4 %copy-start = (f32[1,1,64,2048]{3,2,1,0:T(8,128)S(1)}, f32[1,1,64,2048]{3,2,1,0:T(8,128)}, u32[]{:S(2)}) copy-start(f32[1,1,64,2048]{3,2,1,0:T(8,128)} %param.7) | copy-start | bytes 1572868

commit v5 on v2

--- a/solution.py
+++ b/solution.py
@@ -181,29 +181,27 @@
     x_copies = {}
 
     def products(c):
-        sums = [None] * n_org
+        ceilings, scales, totals = [], [], []
         for r in range(n_org):
             shifted = [tops[b, c] + (reach[r, b] - 1.0) * -FLOOR for b in range(n_dst)]
-            ceiling = functools.reduce(jnp.maximum, shifted)
-            total = None
-            for b in range(n_dst):
-                scale = reach[r, b] * jnp.exp(shifted[b] - ceiling)
-                term = scale * jnp.dot(
-                    kern_in[b, r], wbuf[b, c], preferred_element_type=jnp.float32)
-                total = term if total is None else total + term
-            sums[r] = total
-            if r == 0:
-                own_sum[c] = total
-                own_top[c] = ceiling
-            else:
-                x_out[r - 1, c] = total.astype(jnp.bfloat16)
-                x_out_top[r - 1, c] = ceiling
-                to = lax.rem(q + r, n_org)
-                for i, (src, dst) in enumerate(((x_out_top, x_in_top), (x_out, x_in))):
-                    copy = remote(src.at[r - 1, c], dst.at[r - 1, c],
-                                  x_send.at[r - 1, c, i], x_recv.at[r - 1, c, i], org=to)
-                    copy.start()
-                    x_copies.setdefault(c, []).append(copy)
+            ceilings.append(functools.reduce(jnp.maximum, shifted))
+            scales.append([reach[r, b] * jnp.exp(shifted[b] - ceilings[r]) for b in range(n_dst)])
+        for b in range(n_dst):
+            stacked = kern_in[b].reshape(n_org * rows, rows)
+            product = jnp.dot(stacked, wbuf[b, c], preferred_element_type=jnp.float32)
+            terms = [scales[r][b] * product[r * rows:(r + 1) * rows] for r in range(n_org)]
+            totals = [x + y for x, y in zip(totals, terms)] if b else terms
+        own_sum[c] = totals[0]
+        own_top[c] = ceilings[0]
+        for r in range(1, n_org):
+            x_out[r - 1, c] = totals[r].astype(jnp.bfloat16)
+            x_out_top[r - 1, c] = ceilings[r]
+            to = lax.rem(q + r, n_org)
+            for i, (src, dst) in enumerate(((x_out_top, x_in_top), (x_out, x_in))):
+                copy = remote(src.at[r - 1, c], dst.at[r - 1, c],
+                              x_send.at[r - 1, c, i], x_recv.at[r - 1, c, i], org=to)
+                copy.start()
+                x_copies.setdefault(c, []).append(copy)
 
     def finish(c):
         for copy in x_copies.get(c, []):

time: 35.8 us -> 35.8 us (level)
  no operation moved by 1% of the time
where the time goes in v5:
time: 35.8 us; the launch traced here: 35.6 us
  Pallas kernels  33.7 us (94%)
  other arithmetic  1.89 us (5%)
    pallas_call x1, Pallas kernels, on_device(): pl.pallas_call(functools.partial(sweep, sizes), out_shape=jax.ShapeDtypeS...  33.7 us
    add x1, other arithmetic, on_device(): return utility + partial[None, None]  1.89 us

profile of v5, /device:TPU:0, one launch (start us, length us, event | category | flops | bytes accessed | tf_op | source)
XLA Modules:
  0.0 35.6 jit_solution(11470445080731700980)
XLA Ops:
  0.0 0.0 copy-start
  0.0 33.7 %shard_map.64 = f32[64,2048]{1,0:T(8,128)} custom-call(f32[64,2048]{1,0:T(8,128)} %bitcast.6, f32[4,64,128]{2,1,0:T(8,128)} %bitcast.7, s32[1,4096]{1,0:T(1,128)} %bitcast.8, s32[3,8]{1,0:T(4,128)} %bitcast.9, s32[8]{0:T(128)} %counts_in.1), custom_call_target="tpu_custom_call" | custom-call | tf_op jit(solution)/shard_map/pallas_call | solution.py:268
  33.7 0.0 copy-done
  33.7 1.9 %bitcast_add_fusion = f32[1,1,64,2048]{3,2,1,0:T(8,128)} fusion(f32[1,1,64,2048]{3,2,1,0:T(8,128)S(1)} %copy-done, f32[64,2048]{1,0:T(8,128)} %shard_map.64), kind=kLoop, calls=%fused_computation | loop fusion | flops 131072 | bytes 1572864 | tf_op jit(solution)/shard_map/add | solution.py:310
Async XLA Ops:
  0.0 33.7 %copy-start = (f32[1,1,64,2048]{3,2,1,0:T(8,128)S(1)}, f32[1,1,64,2048]{3,2,1,0:T(8,128)}, u32[]{:S(2)}) copy-start(f32[1,1,64,2048]{3,2,1,0:T(8,128)} %param.7) | copy-start | bytes 1572868
